TPU v7x, 32 devices: a whole 2x2x4 slice. The times are simulated.
32 devices in a mesh: seq: 16 (over z, y, x), head: 2 (over core).
Axes of the slice: x: 2, y: 2, z: 4, core: 2. Of those that a mesh axis runs over, the one named last changes fastest.
Arguments:
- activations: bfloat16 [8192, 2048], P('seq', 'head'), may hold values from -6 to 6
- w_proj: bfloat16 [3, 2048, 2048], P(None, None, 'head'), may hold values from -0.125 to 0.125
- level_weight: float32 [8192, 16, 14], P('seq', 'head'), may hold values from 0.25 to 4
- grad_out: bfloat16 [8192, 2048], P('seq', 'head'), may hold values from -6 to 6
Outputs:
- attn_output: bfloat16 [8192, 2048], P('seq', 'head')
- grad_query: bfloat16 [8192, 2048], P('seq', 'head')
- grad_key: bfloat16 [8192, 2048], P('seq', 'head')
- grad_value: bfloat16 [8192, 2048], P('seq', 'head')
All inputs are finite; a program needn't handle non-finite values.
Results may differ from a plain program's by a relative error of at most 0.0085.
Values may be sent and summed in bfloat16 or wider, within the bound.
A program may use at most 64 MiB of HBM per device.

v0:
```python
import jax
import jax.numpy as jnp
from jax import lax
from jax.sharding import PartitionSpec as P


def partner_2(value, axis, bit):
    return lax.ppermute(value, axis, [(i, i ^ 1 << bit) for i in range(lax.axis_size(axis))])


def bit_length_of(numbers, width):
    total = jnp.zeros_like(numbers)
    for shift_by in range(width):
        total = total + (jnp.right_shift(numbers, shift_by) > 0).astype(jnp.int32)
    return total


def level_factors(count):
    index_list = jnp.arange(count, dtype=jnp.int32)
    return jnp.exp2(-0.5 * (jnp.maximum(index_list, 1) - 1).astype(jnp.float32))


def on_device(activations, w_proj, level_weight, grad_out):
    highest = lax.Precision.HIGHEST
    block_len = activations.shape[0]
    local_width = w_proj.shape[2]
    head_count = level_weight.shape[1]
    head_dim = local_width // head_count
    scale = head_dim ** (-0.5)
    block_bits = block_len.bit_length() - 1
    seq_bits = lax.axis_size("seq").bit_length() - 1
    seq_index = lax.axis_index("seq")
    projected = jnp.einsum(
        "tn,cnf->tcf",
        lax.all_gather(activations, "head", axis=1, tiled=True),
        w_proj,
        preferred_element_type=jnp.float32,
    )
    projected = projected.astype(jnp.bfloat16).reshape(block_len, 3, head_count, head_dim)
    query_rows = projected[:, 0]
    key_rows = projected[:, 1]
    value_rows = projected[:, 2]
    cotangent = grad_out.reshape(block_len, head_count, head_dim)
    weight = level_weight * level_factors(level_weight.shape[2])
    local_pos = jnp.arange(block_len, dtype=jnp.int32)
    local_level = bit_length_of(jnp.bitwise_xor(local_pos[:, None], local_pos[None, :]), block_bits)
    causal = local_pos[None, :] <= local_pos[:, None]
    mask_weight = jnp.zeros((head_count, block_len, block_len), jnp.float32)
    for level_ix in range(block_bits + 1):
        chosen = (local_level == level_ix) & causal
        mask_weight = mask_weight + jnp.where(
            chosen[None], weight[:, :, level_ix].T[:, :, None], 0.0
        )
    scores = (
        jnp.einsum("thd,shd->hts", query_rows, key_rows, preferred_element_type=jnp.float32) * scale
    )
    attn = (scores * mask_weight).astype(jnp.bfloat16)
    out_inner = jnp.einsum("hts,shd->thd", attn, value_rows, preferred_element_type=jnp.float32)
    back = jnp.einsum("thd,shd->hts", cotangent, value_rows, preferred_element_type=jnp.float32)
    grads = (back * mask_weight * scale).astype(jnp.bfloat16)
    dq_inner = jnp.einsum("hts,shd->thd", grads, key_rows, preferred_element_type=jnp.float32)
    dk_inner = jnp.einsum("hts,thd->shd", grads, query_rows, preferred_element_type=jnp.float32)
    dv_inner = jnp.einsum("hts,thd->shd", attn, cotangent, preferred_element_type=jnp.float32)
    cross = weight[:, :, block_bits + 1 :]
    states = jnp.einsum("shx,shy->hxy", key_rows, value_rows, preferred_element_type=jnp.float32)
    weighted = cross[:, :, :, None] * query_rows.astype(jnp.float32)[:, :, None, :]
    level_grads = jnp.einsum(
        "thjx,thy->jhxy", weighted, cotangent.astype(jnp.float32), precision=highest
    )
    bit_flags = [
        (jnp.right_shift(seq_index, bit_index) % 2).astype(jnp.float32)
        for bit_index in range(seq_bits)
    ]
    upward = []
    prefix = None
    group = states
    for bit_index in range(seq_bits):
        partner = partner_2(group.astype(jnp.bfloat16), "seq", bit_index).astype(group.dtype)
        upward.append(partner * bit_flags[bit_index])
        group = group + partner
    prefix = jnp.stack(upward)
    lead = 0
    moving = level_grads
    downward = []
    for bit_index in range(seq_bits):
        partner = partner_2(moving.astype(jnp.bfloat16), "seq", bit_index).astype(moving.dtype)
        downward.append(partner[lead] * (1.0 - bit_flags[bit_index]))
        summed = moving + partner
        moving = jnp.concatenate([summed[:lead], summed[lead + 1 :]], 0)
    prefix_half = prefix.astype(jnp.bfloat16)
    suffix_half = jnp.stack(downward).astype(jnp.bfloat16)
    reads = jnp.einsum(
        "thx,jhxy->thjy", query_rows, prefix_half, preferred_element_type=jnp.float32
    )
    out_cross = scale * jnp.sum(cross[..., None] * reads, 2)
    reads_back = jnp.einsum(
        "thy,jhxy->thjx", cotangent, prefix_half, preferred_element_type=jnp.float32
    )
    dq_cross = scale * jnp.sum(cross[..., None] * reads_back, 2)
    dk_cross = scale * jnp.einsum(
        "shy,jhxy->shx", value_rows, suffix_half, preferred_element_type=jnp.float32
    )
    dv_cross = scale * jnp.einsum(
        "shx,jhxy->shy", key_rows, suffix_half, preferred_element_type=jnp.float32
    )

    def finish(total):
        return total.reshape(block_len, local_width).astype(jnp.bfloat16)

    return (
        finish(out_inner + out_cross),
        finish(dq_inner + dq_cross),
        finish(dk_inner + dk_cross),
        finish(dv_inner + dv_cross),
    )


def solution(mesh):
    in_specs = (P("seq", "head"), P(None, None, "head"), P("seq", "head", None), P("seq", "head"))
    out_specs = (P("seq", "head"), P("seq", "head"), P("seq", "head"), P("seq", "head"))
    return jax.shard_map(
        on_device, mesh=mesh, in_specs=in_specs, out_specs=out_specs, check_vma=False
    )
```

profile of v0, /device:TPU:0, one launch (start us, length us, event | category | flops | bytes accessed | tf_op | source)
XLA Modules:
  0.0 160.8 jit_solution(883111691701707313)
XLA Ops:
  9.0 1.5 copy.75
  10.6 1.6 copy.48
  12.8 1.7 %fusion.24 = (pred[512,512]{1,0:T(8,128)(4,1)S(1)}, pred[512,512]{1,0:T(8,128)(4,1)}) fusion(), kind=kLoop, calls=%fused_computation.39 | loop fusion | flops 10747904 | bytes 524288 | tf_op jit(solution)/shard_map/and | solution.py:50
  14.5 1.8 %fusion.26 = (pred[512,512]{1,0:T(8,128)(4,1)}, pred[512,512]{1,0:T(8,128)(4,1)}) fusion(), kind=kLoop, calls=%fused_computation.41 | loop fusion | flops 10747904 | bytes 524288 | tf_op jit(solution)/shard_map/and | solution.py:50
  16.3 1.8 %fusion.28 = (pred[512,512]{1,0:T(8,128)(4,1)}, pred[512,512]{1,0:T(8,128)(4,1)}) fusion(), kind=kLoop, calls=%fused_computation.43 | loop fusion | flops 10747904 | bytes 524288 | tf_op jit(solution)/shard_map/and | solution.py:50
  18.1 1.8 %fusion.30 = (pred[512,512]{1,0:T(8,128)(4,1)}, pred[512,512]{1,0:T(8,128)(4,1)}) fusion(), kind=kLoop, calls=%fused_computation.45 | loop fusion | flops 10747904 | bytes 524288 | tf_op jit(solution)/shard_map/and | solution.py:50
  20.0 1.8 %fusion.32 = (pred[512,512]{1,0:T(8,128)(4,1)}, pred[512,512]{1,0:T(8,128)(4,1)}) fusion(), kind=kLoop, calls=%fused_computation.47 | loop fusion | flops 10747904 | bytes 524288 | tf_op jit(solution)/shard_map/and | solution.py:50
  22.9 10.4 %convolution_convert_fusion = bf16[512,3,1024]{2,0,1:T(8,128)(2,1)S(1)} fusion(bf16[3,2048,1024]{2,1,0:T(8,128)(2,1)} %param.5, bf16[512,2048]{1,0:T(8,128)(2,1)} %all-gather.2.cloned.1.call-done), kind=kOutput, calls=%fused_computation.13 | convolution fusion | flops 6444023808 | bytes 17825792 | tf_op jit(solution)/shard_map/tn,cnf->tcf/dot_general | solution.py:33
  35.2 1.5 bitcast_convert_fusion
  36.7 2.9 %copy.45 = f32[512,8,128]{0,2,1:T(8,128)} copy(f32[512,8,128]{2,0,1:T(8,128)} %bitcast_convert_fusion) | data formatting | bytes 4194304 | tf_op jit(solution)/shard_map/convert_element_type | solution.py:66
  39.6 1.8 %copy.71 = bf16[512,1,8,128]{0,3,2,1:T(8,128)(2,1)S(1)} copy(bf16[512,1,8,128]{3,2,0,1:T(8,128)(2,1)} %get-tuple-element.17) | data formatting | bytes 2097152
  42.1 1.9 %collective-permute-start = (bf16[8,128,128]{2,1,0:T(8,128)(2,1)S(1)}, bf16[8,128,128]{2,1,0:T(8,128)(2,1)S(1)}, u32[]{:S(2)}, u32[]{:S(2)}) collective-permute-start(bf16[8,128,128]{2,1,0:T(8,128)(2,1)S(1)} %get-tuple-element.35), channel_id=1, source_target_pairs={{0,2},{2,0},{4,6},{6,4},{8,10},{10,8},{12,14},{14,12},{16,18},{18,... | collective-permute-start | bytes 786440 | tf_op jit(solution)/shard_map/ppermute | solution.py:8
  44.0 6.1 %fusion.60 = (bf16[4,8,128,128]{3,2,0,1:T(8,128)(2,1)S(1)}, f32[4,8,128,128]{3,2,0,1:T(8,128)S(1)}) fusion(bf16[512,8,128,1]{2,1,0,3:T(8,128)(2,1)} %bitcast.140, f32[512,8,128]{0,2,1:T(8,128)} %copy.45, f32[512,8,4]{0,2,1:T(4,128)S(1)} %copy.34), kind=kOutput, calls=%fused_computation.110 | convolution fusion | flops 3223846912 | bytes 6356992 | tf_op jit(solution)/shard_map/thjx,thy->jhxy/dot_general | solution.py:67
  50.7 1.8 %collective-permute-start.1 = (bf16[8,128,128]{2,1,0:T(8,128)(2,1)S(1)}, bf16[8,128,128]{2,1,0:T(8,128)(2,1)S(1)}, u32[]{:S(2)}, u32[]{:S(2)}) collective-permute-start(bf16[8,128,128]{2,1,0:T(8,128)(2,1)S(1)} %fusion.50), channel_id=1, source_target_pairs={{0,4},{2,6},{4,0},{6,2},{8,12},{10,14},{12,8},{14,10},{16,20},{18,... | collective-permute-start | bytes 786440 | tf_op jit(solution)/shard_map/ppermute | solution.py:8
  52.6 11.7 %multiply_convert_fusion = bf16[8,512,512]{2,1,0:T(8,128)(2,1)} fusion(f32[8,512]{1,0:T(8,128)S(1)} %get-tuple-element.26, pred[512,512]{1,0:T(8,128)(4,1)S(1)} %get-tuple-element.39, f32[8,512]{1,0:T(8,128)S(1)} %get-tuple-element.27, pred[512,512]{1,0:T(8,128)(4,1)S(1)} %copy-done.7, f32[8,512]{1,0:T(8,128)S(1)} %get-tuple-element.28, ...), kind=kOutput, calls=%fused_computation.9 | convolution fusion | flops 583008256 | bytes 9076736 | tf_op jit(solution)/shard_map/thd,shd->hts/dot_general | solution.py:55
  64.4 1.6 collective-permute-start.2
  66.0 10.9 %fusion.2 = bf16[8,512,512]{2,1,0:T(8,128)(2,1)S(1)} fusion(bf16[512,8,128]{0,2,1:T(8,128)(2,1)S(1)} %copy-done.5, bf16[512,1,8,128]{0,3,2,1:T(8,128)(2,1)S(1)} %copy.71, f32[8,512]{1,0:T(8,128)S(1)} %get-tuple-element.26, pred[512,512]{1,0:T(8,128)(4,1)S(1)} %get-tuple-element.39, f32[8,512]{1,0:T(8,128)S(1)} %get-tuple-element.27, ...), kind=kOutput, calls=%fused_computation.4 | convolution fusion | flops 583008256 | bytes 9076736 | tf_op jit(solution)/shard_map/thd,shd->hts/dot_general | solution.py:59
  77.2 2.6 %collective-permute-start.3 = (bf16[8,128,128]{2,1,0:T(8,128)(2,1)S(1)}, bf16[8,128,128]{2,1,0:T(8,128)(2,1)S(1)}, u32[]{:S(2)}, u32[]{:S(2)}) collective-permute-start(bf16[8,128,128]{2,1,0:T(8,128)(2,1)S(1)} %get-tuple-element.22), channel_id=1, source_target_pairs={{0,16},{2,18},{4,20},{6,22},{8,24},{10,26},{12,28},{14,30},{16,0},... | collective-permute-start | bytes 786440 | tf_op jit(solution)/shard_map/ppermute | solution.py:8
  79.9 2.2 %fusion.16 = f32[8,128,512]{2,1,0:T(8,128)} fusion(bf16[8,512,512]{2,1,0:T(8,128)(2,1)S(1)} %fusion.2, bf16[512,1,8,128]{3,2,0,1:T(8,128)(2,1)S(1)} %get-tuple-element.16), kind=kOutput, calls=%fused_computation.29 | convolution fusion | flops 536870912 | bytes 7340032 | tf_op jit(solution)/shard_map/hts,thd->shd/dot_general | solution.py:62
  82.0 9.1 %collective-permute-done.3 = bf16[8,128,128]{2,1,0:T(8,128)(2,1)S(1)} collective-permute-done((bf16[8,128,128]{2,1,0:T(8,128)(2,1)S(1)}, bf16[8,128,128]{2,1,0:T(8,128)(2,1)S(1)}, u32[]{:S(2)}, u32[]{:S(2)}) %collective-permute-start.3) | collective-permute-done | bytes 262176 | tf_op jit(solution)/shard_map/ppermute | solution.py:8
  91.2 1.6 %convert_element_type.614 = f32[4,8,128,128]{3,2,0,1:T(8,128)} convert(bf16[4,8,128,128]{3,2,0,1:T(8,128)(2,1)S(1)} %collective-permute-done.4) | non-fusion elementwise | flops 524288 | bytes 3145728 | tf_op jit(solution)/shard_map/convert_element_type | solution.py:86
  92.8 1.7 %fusion.57 = (bf16[3,8,128,128]{3,2,0,1:T(8,128)(2,1)S(1)}, f32[3,8,128,128]{3,2,0,1:T(8,128)S(1)}) fusion(f32[4,8,128,128]{3,2,0,1:T(8,128)} %convert_element_type.614, f32[4,8,128,128]{3,2,0,1:T(8,128)S(1)} %get-tuple-element.38), kind=kLoop, calls=%fused_computation.107 | loop fusion | flops 786432 | bytes 5505024 | tf_op jit(solution)/shard_map/convert_element_type | solution.py:86
  96.2 2.5 %fusion.9 = bf16[512,8,128]{0,2,1:T(8,128)(2,1)} fusion(f32[512,8,128]{0,2,1:T(8,128)S(1)} %fusion, bf16[8,512,512]{2,1,0:T(8,128)(2,1)S(1)} %fusion.2, bf16[512,1,8,128]{3,2,0,1:T(8,128)(2,1)S(1)} %get-tuple-element.18), kind=kOutput, calls=%fused_computation.17 | convolution fusion | flops 538443776 | bytes 8388608 | tf_op jit(solution)/shard_map/hts,shd->thd/dot_general | solution.py:61
  98.8 15.3 %collective-permute-done.5 = bf16[3,8,128,128]{3,2,0,1:T(8,128)(2,1)S(1)} collective-permute-done((bf16[3,8,128,128]{3,2,0,1:T(8,128)(2,1)S(1)}, bf16[3,8,128,128]{3,2,0,1:T(8,128)(2,1)S(1)}, u32[]{:S(2)}, u32[]{:S(2)}) %collective-permute-start.5) | collective-permute-done | bytes 786464 | tf_op jit(solution)/shard_map/ppermute | solution.py:8
  116.7 2.7 %fusion.3 = f32[512,8,128]{0,2,1:T(8,128)} fusion(f32[512,8,4]{0,2,1:T(4,128)S(1)} %copy.34, bf16[512,1,8,128]{3,2,0,1:T(8,128)(2,1)S(1)} %get-tuple-element.16, bf16[1,8,128,128]{3,2,1,0:T(8,128)(2,1)S(1)} %fusion.51, bf16[1,8,128,128]{3,2,1,0:T(8,128)(2,1)S(1)} %get-tuple-element.24, bf16[1,8,128,128]{3,2,1,0:T(8,128)(2,1)S(1)} %get-tuple-element.23, ...), kind=kOutput, calls=%fused_computation.6 | convolution fusion | flops 542113792 | bytes 4259840 | tf_op jit(solution)/shard_map/thx,jhxy->thjy/dot_general | solution.py:92
  119.5 2.3 %copy.51 = bf16[512,1024]{1,0:T(8,128)(2,1)} copy(bf16[512,1024]{0,1:T(8,128)(2,1)} %bitcast.142) | data formatting | bytes 2097152
  121.8 4.4 %fusion.10 = bf16[512,8,128]{0,2,1:T(8,128)(2,1)S(1)} fusion(f32[512,8,128]{0,2,1:T(8,128)} %fusion.3, bf16[8,512,512]{2,1,0:T(8,128)(2,1)} %multiply_convert_fusion, bf16[512,1,8,128]{0,3,2,1:T(8,128)(2,1)S(1)} %copy.71), kind=kOutput, calls=%fused_computation.19 | convolution fusion | flops 538443776 | bytes 8388608 | tf_op jit(solution)/shard_map/hts,shd->thd/dot_general | solution.py:58
  127.4 2.6 %collective-permute-done.6 = bf16[2,8,128,128]{3,2,0,1:T(8,128)(2,1)} collective-permute-done((bf16[2,8,128,128]{3,2,0,1:T(8,128)(2,1)}, bf16[2,8,128,128]{3,2,0,1:T(8,128)(2,1)}, u32[]{:S(2)}, u32[]{:S(2)}) %collective-permute-start.6) | collective-permute-done | bytes 524320 | tf_op jit(solution)/shard_map/ppermute | solution.py:8
  135.1 10.5 %collective-permute-done.7 = bf16[1,8,128,128]{3,2,0,1:T(8,128)(2,1)S(1)} collective-permute-done((bf16[1,8,128,128]{3,2,0,1:T(8,128)(2,1)S(1)}, bf16[1,8,128,128]{3,2,0,1:T(8,128)(2,1)S(1)}, u32[]{:S(2)}, u32[]{:S(2)}) %collective-permute-start.7) | collective-permute-done | bytes 262176 | tf_op jit(solution)/shard_map/ppermute | solution.py:8
  146.3 1.7 %fusion.8 = bf16[512,8,128]{0,2,1:T(8,128)(2,1)} fusion(f32[8,128,512]{2,1,0:T(8,128)S(1)} %fusion.38, bf16[512,8,128]{0,2,1:T(8,128)(2,1)S(1)} %copy-done.6, bf16[8,512,512]{2,1,0:T(8,128)(2,1)S(1)} %copy-done), kind=kOutput, calls=%fused_computation.15 | convolution fusion | flops 538443776 | bytes 8388608 | tf_op jit(solution)/shard_map/hts,thd->shd/dot_general | solution.py:63
  148.0 2.3 %copy.53 = bf16[512,1024]{1,0:T(8,128)(2,1)} copy(bf16[512,1024]{0,1:T(8,128)(2,1)} %bitcast.143) | data formatting | bytes 2097152
  151.7 2.3 %copy.52 = bf16[512,1024]{1,0:T(8,128)(2,1)} copy(bf16[512,1024]{0,1:T(8,128)(2,1)} %bitcast.138) | data formatting | bytes 2097152
  (77 shorter events, 19.8 us)
Async XLA Ops:
  7.2 15.7 %all-gather.2.cloned.1.call-start = ((), (), s32[]{:S(2)}) async-start(), calls=%async_computation | async-start | bytes 3145728 | tf_op jit(solution)/shard_map/all_gather | solution.py:35
  10.5 22.7 %copy-start.3 = (bf16[64,8,8,128]{3,2,1,0:T(8,128)(2,1)}, bf16[64,8,8,128]{3,2,1,0:T(8,128)(2,1)S(1)}, u32[]{:S(2)}) copy-start(bf16[64,8,8,128]{3,2,1,0:T(8,128)(2,1)S(1)} %copy.75) | copy-start | bytes 3145732
  41.9 10.6 %copy-start.7 = (pred[512,512]{1,0:T(8,128)(4,1)S(1)}, pred[512,512]{1,0:T(8,128)(4,1)}, u32[]{:S(2)}) copy-start(pred[512,512]{1,0:T(8,128)(4,1)} %get-tuple-element.40) | copy-start | bytes 786436
  41.9 10.6 %copy-start.8 = (pred[512,512]{1,0:T(8,128)(4,1)S(1)}, pred[512,512]{1,0:T(8,128)(4,1)}, u32[]{:S(2)}) copy-start(pred[512,512]{1,0:T(8,128)(4,1)} %get-tuple-element.41) | copy-start | bytes 786436
  41.9 10.6 %copy-start.9 = (pred[512,512]{1,0:T(8,128)(4,1)S(1)}, pred[512,512]{1,0:T(8,128)(4,1)}, u32[]{:S(2)}) copy-start(pred[512,512]{1,0:T(8,128)(4,1)} %get-tuple-element.42) | copy-start | bytes 786436
  42.0 10.5 %copy-start.10 = (pred[512,512]{1,0:T(8,128)(4,1)S(1)}, pred[512,512]{1,0:T(8,128)(4,1)}, u32[]{:S(2)}) copy-start(pred[512,512]{1,0:T(8,128)(4,1)} %get-tuple-element.43) | copy-start | bytes 786436
  42.0 10.5 %copy-start.11 = (pred[512,512]{1,0:T(8,128)(4,1)S(1)}, pred[512,512]{1,0:T(8,128)(4,1)}, u32[]{:S(2)}) copy-start(pred[512,512]{1,0:T(8,128)(4,1)} %get-tuple-element.44) | copy-start | bytes 786436
  42.0 10.5 %copy-start.12 = (pred[512,512]{1,0:T(8,128)(4,1)S(1)}, pred[512,512]{1,0:T(8,128)(4,1)}, u32[]{:S(2)}) copy-start(pred[512,512]{1,0:T(8,128)(4,1)} %get-tuple-element.45) | copy-start | bytes 786436
  42.0 10.5 %copy-start.13 = (pred[512,512]{1,0:T(8,128)(4,1)S(1)}, pred[512,512]{1,0:T(8,128)(4,1)}, u32[]{:S(2)}) copy-start(pred[512,512]{1,0:T(8,128)(4,1)} %get-tuple-element.46) | copy-start | bytes 786436
  42.0 10.5 %copy-start.14 = (pred[512,512]{1,0:T(8,128)(4,1)S(1)}, pred[512,512]{1,0:T(8,128)(4,1)}, u32[]{:S(2)}) copy-start(pred[512,512]{1,0:T(8,128)(4,1)} %get-tuple-element.47) | copy-start | bytes 786436
  42.0 10.5 %copy-start.15 = (pred[512,512]{1,0:T(8,128)(4,1)S(1)}, pred[512,512]{1,0:T(8,128)(4,1)}, u32[]{:S(2)}) copy-start(pred[512,512]{1,0:T(8,128)(4,1)} %get-tuple-element.48) | copy-start | bytes 786436
  42.0 10.5 %copy-start.16 = (f32[8,512]{1,0:T(8,128)S(1)}, f32[8,512]{1,0:T(8,128)}, u32[]{:S(2)}) copy-start(f32[8,512]{1,0:T(8,128)} %get-tuple-element.30) | copy-start | bytes 49156
  42.0 10.5 %copy-start.17 = (f32[8,512]{1,0:T(8,128)S(1)}, f32[8,512]{1,0:T(8,128)}, u32[]{:S(2)}) copy-start(f32[8,512]{1,0:T(8,128)} %get-tuple-element.31) | copy-start | bytes 49156
  42.0 10.5 %copy-start.18 = (f32[8,512]{1,0:T(8,128)S(1)}, f32[8,512]{1,0:T(8,128)}, u32[]{:S(2)}) copy-start(f32[8,512]{1,0:T(8,128)} %get-tuple-element.32) | copy-start | bytes 49156
  42.0 10.5 %copy-start.19 = (f32[8,512]{1,0:T(8,128)S(1)}, f32[8,512]{1,0:T(8,128)}, u32[]{:S(2)}) copy-start(f32[8,512]{1,0:T(8,128)} %get-tuple-element.33) | copy-start | bytes 49156
  42.1 10.5 %copy-start.20 = (f32[8,512]{1,0:T(8,128)S(1)}, f32[8,512]{1,0:T(8,128)}, u32[]{:S(2)}) copy-start(f32[8,512]{1,0:T(8,128)} %get-tuple-element.34) | copy-start | bytes 49156
  42.1 8.6 %collective-permute-start = (bf16[8,128,128]{2,1,0:T(8,128)(2,1)S(1)}, bf16[8,128,128]{2,1,0:T(8,128)(2,1)S(1)}, u32[]{:S(2)}, u32[]{:S(2)}) collective-permute-start(bf16[8,128,128]{2,1,0:T(8,128)(2,1)S(1)} %get-tuple-element.35), channel_id=1, source_target_pairs={{0,2},{2,0},{4,6},{6,4},{8,10},{10,8},{12,14},{14,12},{16,18},{18,... | collective-permute-start | bytes 786440 | tf_op jit(solution)/shard_map/ppermute | solution.py:8
  50.1 41.1 %collective-permute-start.4 = (bf16[4,8,128,128]{3,2,0,1:T(8,128)(2,1)S(1)}, bf16[4,8,128,128]{3,2,0,1:T(8,128)(2,1)S(1)}, u32[]{:S(2)}, u32[]{:S(2)}) collective-permute-start(bf16[4,8,128,128]{3,2,0,1:T(8,128)(2,1)S(1)} %get-tuple-element.37), channel_id=1, source_target_pairs={{0,2},{2,0},{4,6},{6,4},{8,10},{10,8},{12,14},{14,12},{16,18},{18,... | collective-permute-start | bytes 3145736 | tf_op jit(solution)/shard_map/ppermute | solution.py:8
  50.7 13.6 %collective-permute-start.1 = (bf16[8,128,128]{2,1,0:T(8,128)(2,1)S(1)}, bf16[8,128,128]{2,1,0:T(8,128)(2,1)S(1)}, u32[]{:S(2)}, u32[]{:S(2)}) collective-permute-start(bf16[8,128,128]{2,1,0:T(8,128)(2,1)S(1)} %fusion.50), channel_id=1, source_target_pairs={{0,4},{2,6},{4,0},{6,2},{8,12},{10,14},{12,8},{14,10},{16,20},{18,... | collective-permute-start | bytes 786440 | tf_op jit(solution)/shard_map/ppermute | solution.py:8
  52.6 13.4 %copy-start.5 = (bf16[512,8,128]{0,2,1:T(8,128)(2,1)S(1)}, bf16[512,8,128]{0,2,1:T(8,128)(2,1)}, u32[]{:S(2)}) copy-start(bf16[512,8,128]{0,2,1:T(8,128)(2,1)} %copy.48) | copy-start | bytes 3145732
  64.4 12.5 %collective-permute-start.2 = (bf16[8,128,128]{2,1,0:T(8,128)(2,1)S(1)}, bf16[8,128,128]{2,1,0:T(8,128)(2,1)S(1)}, u32[]{:S(2)}, u32[]{:S(2)}) collective-permute-start(bf16[8,128,128]{2,1,0:T(8,128)(2,1)S(1)} %fusion.55), channel_id=1, source_target_pairs={{0,8},{2,10},{4,12},{6,14},{8,0},{10,2},{12,4},{14,6},{16,24},{18,... | collective-permute-start | bytes 786440 | tf_op jit(solution)/shard_map/ppermute | solution.py:8
  77.2 13.9 %collective-permute-start.3 = (bf16[8,128,128]{2,1,0:T(8,128)(2,1)S(1)}, bf16[8,128,128]{2,1,0:T(8,128)(2,1)S(1)}, u32[]{:S(2)}, u32[]{:S(2)}) collective-permute-start(bf16[8,128,128]{2,1,0:T(8,128)(2,1)S(1)} %get-tuple-element.22), channel_id=1, source_target_pairs={{0,16},{2,18},{4,20},{6,22},{8,24},{10,26},{12,28},{14,30},{16,0},... | collective-permute-start | bytes 786440 | tf_op jit(solution)/shard_map/ppermute | solution.py:8
  91.2 3.8 %copy-start.4 = (bf16[64,8,8,128]{3,2,1,0:T(8,128)(2,1)S(1)}, bf16[64,8,8,128]{3,2,1,0:T(8,128)(2,1)}, u32[]{:S(2)}) copy-start(bf16[64,8,8,128]{3,2,1,0:T(8,128)(2,1)} %copy-done.3) | copy-start | bytes 3145732
  94.6 19.5 %collective-permute-start.5 = (bf16[3,8,128,128]{3,2,0,1:T(8,128)(2,1)S(1)}, bf16[3,8,128,128]{3,2,0,1:T(8,128)(2,1)S(1)}, u32[]{:S(2)}, u32[]{:S(2)}) collective-permute-start(bf16[3,8,128,128]{3,2,0,1:T(8,128)(2,1)S(1)} %get-tuple-element.14), channel_id=1, source_target_pairs={{0,4},{2,6},{4,0},{6,2},{8,12},{10,14},{12,8},{14,10},{16,20},{18,... | collective-permute-start | bytes 2359304 | tf_op jit(solution)/shard_map/ppermute | solution.py:8
  114.3 1.1 copy-start.2
  116.7 13.3 %collective-permute-start.6 = (bf16[2,8,128,128]{3,2,0,1:T(8,128)(2,1)}, bf16[2,8,128,128]{3,2,0,1:T(8,128)(2,1)}, u32[]{:S(2)}, u32[]{:S(2)}) collective-permute-start(bf16[2,8,128,128]{3,2,0,1:T(8,128)(2,1)} %get-tuple-element.12), channel_id=1, source_target_pairs={{0,8},{2,10},{4,12},{6,14},{8,0},{10,2},{12,4},{14,6},{16,24},{18,... | collective-permute-start | bytes 1572872 | tf_op jit(solution)/shard_map/ppermute | solution.py:8
  131.2 15.1 %copy-start = (bf16[8,512,512]{2,1,0:T(8,128)(2,1)S(1)}, bf16[8,512,512]{2,1,0:T(8,128)(2,1)}, u32[]{:S(2)}) copy-start(bf16[8,512,512]{2,1,0:T(8,128)(2,1)} %multiply_convert_fusion) | copy-start | bytes 12582916
  131.2 15.1 %copy-start.6 = (bf16[512,8,128]{0,2,1:T(8,128)(2,1)S(1)}, bf16[512,8,128]{0,2,1:T(8,128)(2,1)}, u32[]{:S(2)}) copy-start(bf16[512,8,128]{0,2,1:T(8,128)(2,1)} %copy.48) | copy-start | bytes 3145732
  132.5 13.0 %collective-permute-start.7 = (bf16[1,8,128,128]{3,2,0,1:T(8,128)(2,1)S(1)}, bf16[1,8,128,128]{3,2,0,1:T(8,128)(2,1)S(1)}, u32[]{:S(2)}, u32[]{:S(2)}) collective-permute-start(bf16[1,8,128,128]{3,2,0,1:T(8,128)(2,1)S(1)} %get-tuple-element.20), channel_id=1, source_target_pairs={{0,16},{2,18},{4,20},{6,22},{8,24},{10,26},{12,28},{14,30},{16,0},... | collective-permute-start | bytes 786440 | tf_op jit(solution)/shard_map/ppermute | solution.py:8
  146.3 4.0 %copy-start.1 = (f32[8,128,512]{2,1,0:T(8,128)S(1)}, f32[8,128,512]{2,1,0:T(8,128)}, u32[]{:S(2)}) copy-start(f32[8,128,512]{2,1,0:T(8,128)} %fusion.16) | copy-start | bytes 6291460
Sparse Core Ops, SparseCore 0:
  9.5 13.2 all-gather.1
where the time goes:
time: 161 us
  matrix products  56.3 us (35%)
  waiting for transfers between devices  39.4 us (24%)
  other arithmetic  22 us (14%)
  local copies, waits for them, and re-layouts  19.8 us (12%)
  between operations  14.6 us (9%)
  starting transfers between devices  8.81 us (5%)
    ppermute x8, waiting for transfers between devices, partner_2(): lax.ppermute(value, axis, [(i, i ^ 1 << bit) for i in range(lax.axis_size...  37.6 us
    unnamed x49, local copies, waits for them, and re-layouts  13.4 us
    dot_general x1, matrix products, on_device(): jnp.einsum('thd,shd->hts', query_rows, key_rows, preferred_element_type=j...  11.7 us
    dot_general x1, matrix products, on_device(): jnp.einsum('thd,shd->hts', cotangent, value_rows, preferred_element_type=...  10.9 us
    dot_general x1, matrix products, on_device(): jnp.einsum('tn,cnf->tcf', lax.all_gather(activations, 'head', axis=1, til...  10.4 us
    and x5, other arithmetic, on_device(): chosen = (local_level == level_ix) & causal  9.02 us
    ppermute x8, starting transfers between devices, partner_2(): lax.ppermute(value, axis, [(i, i ^ 1 << bit) for i in range(lax.axis_size...  8.78 us
    dot_general x1, matrix products, on_device(): jnp.einsum('thjx,thy->jhxy', weighted, cotangent.astype(jnp.float32), pre...  6.09 us
  transfers between devices with their start and end apart: 9, of which 6 were waited for; matrix products, arithmetic and copies ran while one was open for 39% of the time, Pallas kernels for 0%

commit v1 on v0

v1 whole, which is shorter than its diff:
```python
import functools

import jax
import jax.numpy as jnp
from jax import lax
from jax.experimental import pallas as pl
from jax.experimental.pallas import tpu as pltpu
from jax.sharding import PartitionSpec as P

MESH = pl.DeviceIdType.MESH
F32 = jnp.float32
BF16 = jnp.bfloat16


def dot_nn(a, b):
    return lax.dot_general(a, b, (((1,), (0,)), ((), ())), preferred_element_type=F32)


def dot_nt(a, b):
    return lax.dot_general(a, b, (((1,), (1,)), ((), ())), preferred_element_type=F32)


def dot_tn(a, b):
    return lax.dot_general(a, b, (((0,), (0,)), ((), ())), preferred_element_type=F32)


def level_factor(level):
    return 2.0 ** (-0.5 * (max(level, 1) - 1))


def diagonal_mask(columns, row, size, leaf, position):
    if size == leaf:
        base, difference = position
        total = jnp.zeros((leaf, leaf), F32)
        for level in range(leaf.bit_length()):
            column = columns[row : row + leaf, level : level + 1]
            total = jnp.where(base == level, column, total)
        return total
    half = size // 2
    upper = diagonal_mask(columns, row, half, leaf, position)
    lower = diagonal_mask(columns, row + half, half, leaf, position)
    level = half.bit_length()
    side = jnp.broadcast_to(columns[row + half : row + size, level : level + 1], (half, half))
    return jnp.concatenate(
        [
            jnp.concatenate([upper, jnp.zeros((half, half), F32)], 1),
            jnp.concatenate([side, lower], 1),
        ],
        0,
    )


def kernel(
    dims,
    act_ref,
    w_ref,
    lw_ref,
    cot_ref,
    out_ref,
    dq_ref,
    dk_ref,
    dv_ref,
    acts,
    w_vm,
    cot,
    wcol,
    qkv,
    wq,
    group,
    rgrad,
    moving,
    s_send,
    s_recv,
    r_send,
    r_recv,
    upper,
    inner,
    act_sem,
    cot_sem,
    w_sem,
    act_send_sem,
    act_recv_sem,
    s_send_sem,
    s_recv_sem,
    r_send_sem,
    r_recv_sem,
):
    n_seq, n_head, heads, head_dim, block, features, per = dims
    chunks = heads // per
    bits = n_seq.bit_length() - 1
    block_bits = block.bit_length() - 1
    scale = head_dim**-0.5
    width = per * head_dim
    seq = lax.axis_index("seq")
    head = lax.axis_index("head")
    bit_of = [lax.rem(seq // (1 << j), 2) for j in range(bits)]
    partner_of = [seq + (1 << j) - 2 * (1 << j) * bit_of[j] for j in range(bits)]

    def weight_copy(chunk):
        return pltpu.make_async_copy(
            w_ref.at[:, :, pl.ds(pl.multiple_of(chunk * width, width), width)],
            w_vm.at[chunk],
            w_sem.at[chunk],
        )

    own = pltpu.make_async_copy(act_ref, acts.at[0], act_sem)
    own.start()
    weight_copy(0).start()
    cot_copy = pltpu.make_async_copy(cot_ref, cot, cot_sem)
    cot_copy.start()

    barrier = pltpu.get_barrier_semaphore()
    for r in range(1, n_head):
        pl.semaphore_signal(
            barrier, inc=1, device_id=(seq, lax.rem(head + r, n_head)), device_id_type=MESH
        )
    for j in range(bits):
        pl.semaphore_signal(barrier, inc=1, device_id=(partner_of[j], head), device_id_type=MESH)
    pl.semaphore_wait(barrier, n_head - 1 + bits)

    def act_copy(r):
        return pltpu.make_async_remote_copy(
            src_ref=act_ref,
            dst_ref=acts.at[r],
            send_sem=act_send_sem.at[r],
            recv_sem=act_recv_sem.at[r],
            device_id=(seq, lax.rem(head + r, n_head)),
            device_id_type=MESH,
        )

    for r in range(1, n_head):
        act_copy(r).start()
    for chunk in range(1, chunks):
        weight_copy(chunk).start()

    levels = lw_ref.shape[0]
    for h in range(heads):
        table = jnp.concatenate(
            [lw_ref[level, h : h + 1, :] * (scale * level_factor(level)) for level in range(levels)]
            + [jnp.zeros((1, block), F32)] * (-levels % 8),
            0,
        )
        wcol[h] = table.T

    def s_copy(stage, chunk):
        return pltpu.make_async_remote_copy(
            src_ref=s_send.at[stage, chunk],
            dst_ref=s_recv.at[stage, chunk],
            send_sem=s_send_sem.at[stage, chunk],
            recv_sem=s_recv_sem.at[stage, chunk],
            device_id=(partner_of[stage], head),
            device_id_type=MESH,
        )

    def r_copy(stage, chunk):
        return pltpu.make_async_remote_copy(
            src_ref=r_send.at[stage, chunk],
            dst_ref=r_recv.at[stage, chunk],
            send_sem=r_send_sem.at[stage, chunk],
            recv_sem=r_recv_sem.at[stage, chunk],
            device_id=(partner_of[bits - 1 - stage], head),
            device_id_type=MESH,
        )

    top = bit_of[bits - 1]

    def start_stage(stage, chunk):
        def send_s():
            s_send[stage, chunk] = group[chunk].astype(BF16)
            s_copy(stage, chunk).start()

        def send_r():
            bit = bits - 1 - stage
            term = rgrad[chunk, :, bit]
            if stage == 0:
                r_send[stage, chunk] = term.astype(BF16)
            else:
                flag = bit_of[bit].astype(F32)
                r_send[stage, chunk] = (moving[chunk] + flag * term).astype(BF16)
            r_copy(stage, chunk).start()

        if stage == bits - 1:
            pl.when(top == 0)(send_s)
        else:
            send_s()
        if stage == 0:
            pl.when(top == 1)(send_r)
        else:
            send_r()

    def finish_stage(stage, chunk):
        rows = pl.ds(stage * head_dim, head_dim)

        if stage == bits - 1:

            @pl.when(top == 1)
            def _():
                s_copy(stage, chunk).wait_recv()
                upper[chunk, :, rows, :] = s_recv[stage, chunk]

            @pl.when(top == 0)
            def _():
                upper[chunk, :, rows, :] = jnp.zeros((per, head_dim, head_dim), BF16)

        else:
            s_copy(stage, chunk).wait_recv()
            got = s_recv[stage, chunk].astype(F32)
            upper[chunk, :, rows, :] = (got * bit_of[stage].astype(F32)).astype(BF16)
            group[chunk] += got

        if stage == 0:

            @pl.when(top == 0)
            def _():
                r_copy(stage, chunk).wait_recv()
                moving[chunk] = r_recv[stage, chunk].astype(F32)

            @pl.when(top == 1)
            def _():
                moving[chunk] = jnp.zeros((per, head_dim, head_dim), F32)

        else:
            r_copy(stage, chunk).wait_recv()
            moving[chunk] += r_recv[stage, chunk].astype(F32)

    def tick(time):
        for stage in range(bits + 1):
            chunk = time - stage

            @pl.when((chunk >= 0) & (chunk < chunks))
            def _():
                if stage > 0:
                    finish_stage(stage - 1, chunk)
                if stage < bits:
                    start_stage(stage, chunk)

    own.wait()
    offsets = [
        pl.multiple_of(lax.rem(head + n_head - r, n_head) * features, features)
        for r in range(n_head)
    ]

    def project(chunk, _):
        weight_copy(chunk).wait()

        @pl.when(chunk == 0)
        def _():
            cot_copy.wait()
            for r in range(1, n_head):
                act_copy(r).wait_recv()

        for c in (1, 2, 0):
            total = dot_nn(acts[0], w_vm[chunk, c, pl.ds(offsets[0], features), :])
            for r in range(1, n_head):
                total += dot_nn(acts[r], w_vm[chunk, c, pl.ds(offsets[r], features), :])
            total = total.astype(BF16)
            for i in range(per):
                qkv[c, chunk * per + i] = total[:, i * head_dim : (i + 1) * head_dim]
        for i in range(per):
            h = chunk * per + i
            group[chunk, i] = dot_tn(qkv[1, h], qkv[2, h])
            query = qkv[0, h].astype(F32)
            columns = wcol[h]
            for j in range(bits):
                level = block_bits + 1 + j
                wq[h, :, j * head_dim : (j + 1) * head_dim] = (
                    query * columns[:, level : level + 1]
                ).astype(BF16)
            lanes = pl.ds(pl.multiple_of(h * head_dim, head_dim), head_dim)
            grads = dot_tn(cot[:, lanes], wq[h])
            for j in range(bits):
                rgrad[chunk, i, j] = grads[:, j * head_dim : (j + 1) * head_dim]
        tick(chunk)
        return 0

    lax.fori_loop(0, chunks, project, 0)

    tile = min(2 * head_dim, block)
    leaf = min(head_dim, tile)
    tiles = block // tile
    row_ids = lax.broadcasted_iota(jnp.int32, (leaf, leaf), 0)
    col_ids = lax.broadcasted_iota(jnp.int32, (leaf, leaf), 1)
    differ = jnp.bitwise_xor(row_ids, col_ids)
    leaf_level = jnp.zeros((leaf, leaf), jnp.int32)
    for shift in range(leaf.bit_length() - 1):
        leaf_level = leaf_level + (differ >= (1 << shift)).astype(jnp.int32)
    leaf_level = jnp.where(col_ids <= row_ids, leaf_level, -1)

    def attend(h):
        lanes = pl.ds(pl.multiple_of(h * head_dim, head_dim), head_dim)
        columns = wcol[h]
        for b in range(tiles):
            first = b * tile
            query = qkv[0, h, first:, :]
            key = qkv[1, h, first : first + tile, :]
            value = qkv[2, h, first : first + tile, :]
            cotangent = cot[first:, lanes]
            mask = [diagonal_mask(columns, first, tile, leaf, (leaf_level, differ))]
            for a in range(b + 1, tiles):
                level = tile.bit_length() - 1 + (a ^ b).bit_length()
                column = columns[a * tile : (a + 1) * tile, level : level + 1]
                mask.append(jnp.broadcast_to(column, (tile, tile)))
            mask = jnp.concatenate(mask, 0) if len(mask) > 1 else mask[0]
            attn = (dot_nt(query, key) * mask).astype(BF16)
            grads = (dot_nt(cotangent, value) * mask).astype(BF16)
            out_part = dot_nn(attn, value)
            dq_part = dot_nn(grads, key)
            if b == 0:
                inner[0, h] = out_part
                inner[1, h] = dq_part
            else:
                inner[0, h, first:, :] += out_part
                inner[1, h, first:, :] += dq_part
            inner[2, h, first : first + tile, :] = dot_tn(grads, query)
            inner[3, h, first : first + tile, :] = dot_tn(attn, cotangent)

    def middle(chunk, _):
        tick(chunks + chunk)
        for i in range(per):
            attend(chunk * per + i)
        return 0

    lax.fori_loop(0, chunks, middle, 0)
    for time in range(2 * chunks, chunks + bits):
        tick(time)

    def cross(chunk, _):
        for i in range(per):
            h = chunk * per + i
            lanes = pl.ds(pl.multiple_of(h * head_dim, head_dim), head_dim)
            columns = wcol[h]
            states = upper[chunk, i]
            out_ref[:, lanes] = (inner[0, h] + dot_nn(wq[h], states)).astype(BF16)
            back = dot_nt(cot[:, lanes], states)
            total = inner[1, h]
            for j in range(bits):
                level = block_bits + 1 + j
                total += (
                    back[:, j * head_dim : (j + 1) * head_dim] * columns[:, level : level + 1]
                )
            dq_ref[:, lanes] = total.astype(BF16)
            suffix = moving[chunk, i].astype(BF16)
            dk_ref[:, lanes] = (inner[2, h] + dot_nn(qkv[2, h], suffix)).astype(BF16)
            dv_ref[:, lanes] = (inner[3, h] + dot_nt(qkv[1, h], suffix)).astype(BF16)
        return 0

    lax.fori_loop(0, chunks, cross, 0)

    for r in range(1, n_head):
        act_copy(r).wait_send()

    def drain(chunk, _):
        for stage in range(bits):
            if stage == bits - 1:
                pl.when(top == 0)(lambda: s_copy(stage, chunk).wait_send())
            else:
                s_copy(stage, chunk).wait_send()
            if stage == 0:
                pl.when(top == 1)(lambda: r_copy(stage, chunk).wait_send())
            else:
                r_copy(stage, chunk).wait_send()
        return 0

    lax.fori_loop(0, chunks, drain, 0)


def on_device(n_seq, n_head, activations, w_proj, level_weight, grad_out):
    block, features = activations.shape
    width = w_proj.shape[2]
    heads = level_weight.shape[1]
    head_dim = width // heads
    per = 2 if heads % 2 == 0 else 1
    chunks = heads // per
    bits = n_seq.bit_length() - 1
    levels = level_weight.shape[2]
    padded = levels + (-levels % 8)
    dims = (n_seq, n_head, heads, head_dim, block, features, per)
    square = (head_dim, head_dim)
    result = jax.ShapeDtypeStruct((block, width), BF16)
    dma = pltpu.SemaphoreType.DMA
    any_spec = pl.BlockSpec(memory_space=pl.ANY)
    vmem_spec = pl.BlockSpec(memory_space=pltpu.VMEM)
    return pl.pallas_call(
        functools.partial(kernel, dims),
        out_shape=[result] * 4,
        in_specs=[any_spec, any_spec, vmem_spec, any_spec],
        out_specs=[vmem_spec] * 4,
        scratch_shapes=[
            pltpu.VMEM((n_head, block, features), BF16),
            pltpu.VMEM((chunks, 3, w_proj.shape[1], per * head_dim), BF16),
            pltpu.VMEM((block, width), BF16),
            pltpu.VMEM((heads, block, padded), F32),
            pltpu.VMEM((3, heads, block, head_dim), BF16),
            pltpu.VMEM((heads, block, bits * head_dim), BF16),
            pltpu.VMEM((chunks, per) + square, F32),
            pltpu.VMEM((chunks, per, bits) + square, F32),
            pltpu.VMEM((chunks, per) + square, F32),
            pltpu.VMEM((bits, chunks, per) + square, BF16),
            pltpu.VMEM((bits, chunks, per) + square, BF16),
            pltpu.VMEM((bits, chunks, per) + square, BF16),
            pltpu.VMEM((bits, chunks, per) + square, BF16),
            pltpu.VMEM((chunks, per, bits * head_dim, head_dim), BF16),
            pltpu.VMEM((4, heads, block, head_dim), F32),
            dma,
            dma,
            dma((chunks,)),
            dma((n_head,)),
            dma((n_head,)),
            dma((bits, chunks)),
            dma((bits, chunks)),
            dma((bits, chunks)),
            dma((bits, chunks)),
        ],
        compiler_params=pltpu.CompilerParams(
            collective_id=0, has_side_effects=True, vmem_limit_bytes=56 * 2**20
        ),
    )(activations, w_proj, jnp.transpose(level_weight, (2, 1, 0)), grad_out)


def solution(mesh):
    in_specs = (P("seq", "head"), P(None, None, "head"), P("seq", "head", None), P("seq", "head"))
    out_specs = (P("seq", "head"), P("seq", "head"), P("seq", "head"), P("seq", "head"))
    return jax.shard_map(
        functools.partial(on_device, mesh.shape["seq"], mesh.shape["head"]),
        mesh=mesh,
        in_specs=in_specs,
        out_specs=out_specs,
        check_vma=False,
    )
```

time: 161 us -> 56.2 us (0.35)
  matrix products: 56.3 us -> 0 us
  Pallas kernels: 0 us -> 46.2 us
  waiting for transfers between devices: 39.4 us -> 0 us
  other arithmetic: 22 us -> 0 us
  between operations: 14.6 us -> 0.64 us
  local copies, waits for them, and re-layouts: 19.8 us -> 9.05 us
  starting transfers between devices: 8.81 us -> 0 us
    dot_general x13 -> x0, matrix products: 56.3 us -> none  [the longest x1 11.7 us: on_device(): jnp.einsum('thd,shd->hts', query_rows, key_rows, preferred_element_type=j...]
    pallas_call x0 -> x1, Pallas kernels: none -> 46.2 us  [on_device(): pl.pallas_call(functools.partial(kernel, dims), out_shape=[result] * 4, i...]
    ppermute x8 -> x0, waiting for transfers between devices: 37.6 us -> none  [partner_2(): lax.ppermute(value, axis, [(i, i ^ 1 << bit) for i in range(lax.axis_size...]
    and x5 -> x0, other arithmetic: 9.02 us -> none  [on_device(): chosen = (local_level == level_ix) & causal]
    ppermute x8 -> x0, starting transfers between devices: 8.78 us -> none  [partner_2(): lax.ppermute(value, axis, [(i, i ^ 1 << bit) for i in range(lax.axis_size...]
    convert_element_type x8 -> x0, other arithmetic: 7.61 us -> none  [the longest x2 3.04 us: on_device(): moving.astype(jnp.bfloat16)]
    unnamed x49 -> x4, local copies, waits for them, and re-layouts: 13.4 us -> 9.05 us
    another operation x6 -> x0, other arithmetic: 4.21 us -> none
  transfers between devices with their start and end apart: 9 -> 0, of which waited for: 6 -> 0; matrix products, arithmetic and copies ran while one was open for 39% -> 0% of each run, Pallas kernels for 0% -> 0%
where the time goes in v1:
time: 56.2 us; the launch traced here: 55.9 us
  Pallas kernels  46.2 us (82%)
  local copies, waits for them, and re-layouts  9.05 us (16%)
  between operations  0.64 us (1%)
    pallas_call x1, Pallas kernels, on_device(): pl.pallas_call(functools.partial(kernel, dims), out_shape=[result] * 4, i...  46.2 us
    unnamed x4, local copies, waits for them, and re-layouts  9.05 us

profile of v1, /device:TPU:0, one launch (start us, length us, event | category | flops | bytes accessed | tf_op | source)
XLA Modules:
  0.0 55.9 jit_solution(17207258361915494157)
XLA Ops:
  0.6 46.2 %shard_map.75 = (bf16[512,1024]{1,0:T(8,128)(2,1)}, bf16[512,1024]{1,0:T(8,128)(2,1)}, bf16[512,1024]{1,0:T(8,128)(2,1)}, bf16[512,1024]{1,0:T(8,128)(2,1)}) custom-call(bf16[512,1024]{1,0:T(8,128)(2,1)} %act_ref.1, bf16[3,2048,1024]{2,1,0:T(8,128)(2,1)} %w_ref.1, f32[14,8,512]{2,1,0:T(8,128)} %bitcast.1, bf16[512,1024]{1,0:T(8,128)(2,1)} %cot_ref.1), custom_call_target="tpu_custom_call" | custom-call | tf_op jit(solution)/shard_map/pallas_call | solution.py:383
  46.9 2.3 %copy.12 = bf16[512,1024]{1,0:T(8,128)(2,1)} copy(bf16[512,1024]{1,0:T(8,128)(2,1)} %get-tuple-element.8) | data formatting | bytes 2097152
  49.1 2.3 %copy.13 = bf16[512,1024]{1,0:T(8,128)(2,1)} copy(bf16[512,1024]{1,0:T(8,128)(2,1)} %get-tuple-element.9) | data formatting | bytes 2097152
  51.4 2.3 %copy.14 = bf16[512,1024]{1,0:T(8,128)(2,1)} copy(bf16[512,1024]{1,0:T(8,128)(2,1)} %get-tuple-element.10) | data formatting | bytes 2097152
  53.6 2.3 %copy.15 = bf16[512,1024]{1,0:T(8,128)(2,1)} copy(bf16[512,1024]{1,0:T(8,128)(2,1)} %get-tuple-element.11) | data formatting | bytes 2097152
